TPU v7x, 32 devices: a whole 2x2x4 slice. The times are simulated.
32 devices in a mesh: groups: 2 (over y), mp: 8 (over z, x), dp: 2 (over core).
Axes of the slice: x: 2, y: 2, z: 4, core: 2. Of those that a mesh axis runs over, the one named last changes fastest.
Arguments:
- inputs: bfloat16 [2048, 8192], P(('groups', 'dp'), 'mp'), parts along dimension 0, may hold values from -6 to 6
- rounding: bfloat16 [16384, 1024], P(('groups', 'dp'), 'mp'), parts along dimension 0, may hold values from -8 to 8
- codes: int32 [16384, 1024], P(('groups', 'dp'), 'mp'), parts along dimension 0, may hold values from 0 to 15
- scales: float32 [128, 8], P(('groups', 'dp'), 'mp'), parts along dimension 0, may hold values from 0.002 to 0.006
- pick: int32 [128, 8], P(('groups', 'dp'), 'mp'), parts along dimension 0, may hold values from 0 to 1
- target: bfloat16 [2048, 2048], P(('groups', 'dp'), 'mp'), parts along dimension 0, may hold values from -6 to 6
Outputs:
- grad: bfloat16 [16384, 1024], P(('groups', 'dp'), 'mp'), parts along dimension 0
There are 2 independent parts, one for each index of `groups`. A program takes and returns all parts, laid end to end along the dimension named above; each array names one. Nothing has to cross between parts.
All inputs are finite; a program needn't handle non-finite values.
Results may differ from a plain program's by a relative error of at most 0.0085.
Values may be sent and summed in bfloat16 or wider, within the bound.
A program may use at most 64 MiB of HBM per device.

v0:
```python
import math

import jax
import jax.numpy as jnp
from jax import lax
from jax.sharding import PartitionSpec as P

BLK = 128


def expand_blocks(table, rows, cols):
    row_blocks, col_blocks = table.shape
    spread = jnp.broadcast_to(table[:, None, :, None], (row_blocks, BLK, col_blocks, BLK))
    return spread.reshape(rows, cols)


def soft_weights(rounding, codes, scales, pick):
    rows, half = rounding.shape
    nblocks = half // BLK
    levels = (codes - 8).astype(jnp.float32)
    soft = jax.nn.sigmoid(rounding.astype(jnp.float32))
    factor = expand_blocks(scales, rows, half)
    kept_weight = (factor * jnp.clip(levels + soft, -8.0, 7.0)).astype(jnp.bfloat16)
    chosen = expand_blocks(pick, rows, half).reshape(rows, nblocks, 1, BLK)
    places = jnp.arange(2, dtype=jnp.int32).reshape(1, 1, 2, 1)
    spread = jnp.broadcast_to(kept_weight.reshape(rows, nblocks, 1, BLK), (rows, nblocks, 2, BLK))
    weight = jnp.where(chosen == places, spread, jnp.zeros((), jnp.bfloat16)).reshape(
        rows, 2 * half
    )
    slope = soft * (1.0 - soft) * (levels < 6.5).astype(jnp.float32)
    return (weight, slope, chosen)


def compact(full, chosen):
    rows = full.shape[0]
    nblocks = chosen.shape[1]
    pieces = full.reshape(rows, nblocks, 2, BLK)
    return jnp.where(chosen[:, :, 0, :] == 0, pieces[:, :, 0, :], pieces[:, :, 1, :]).reshape(
        rows, nblocks * BLK
    )


def body(inputs, rounding, codes, scales, pick, target):
    weight, slope, chosen = soft_weights(rounding, codes, scales, pick)
    tok_rows = inputs.shape[0]
    scale_root = math.sqrt(tok_rows * lax.axis_size("dp"))
    gathered = lax.all_gather(inputs, "mp", axis=1, tiled=True)
    columns = gathered
    outputs = jnp.dot(
        columns,
        lax.all_gather(weight, "dp", axis=0, tiled=True),
        preferred_element_type=jnp.float32,
    )
    resid = ((outputs - target.astype(jnp.float32)) / scale_root).astype(jnp.bfloat16)
    columns = gathered
    weight_grad = lax.psum_scatter(
        lax.dot_general(
            columns, resid, (((0,), (0,)), ((), ())), preferred_element_type=jnp.float32
        ).astype(jnp.bfloat16),
        "dp",
        scatter_dimension=0,
        tiled=True,
    ).astype(jnp.float32)
    return (compact(weight_grad, chosen) * slope).astype(jnp.bfloat16)


def solution(mesh):
    in_specs = (
        P(("groups", "dp"), "mp"),
        P(("groups", "dp"), "mp"),
        P(("groups", "dp"), "mp"),
        P(("groups", "dp"), "mp"),
        P(("groups", "dp"), "mp"),
        P(("groups", "dp"), "mp"),
    )
    out_specs = P(("groups", "dp"), "mp")
    return jax.shard_map(body, mesh=mesh, in_specs=in_specs, out_specs=out_specs, check_vma=False)
```

profile of v0, /device:TPU:0, one launch (start us, length us, event | category | flops | bytes accessed | tf_op | source)
XLA Modules:
  0.0 207.1 jit_solution(16992007690005694910)
XLA Ops:
  6.5 0.0 copy-start
  6.5 0.0 all-gather.3.cloned.1.call-start
  6.5 0.7 broadcast_bitcast_fusion.1
  7.3 0.0 copy-done
  7.3 0.1 broadcast_bitcast_fusion
  7.3 2.2 %multiply_convert_fusion = bf16[4096,128]{1,0:T(8,128)(2,1)S(1)} fusion(s32[4096,128]{1,0:T(8,128)} %param.8, f32[4096]{0:T(1024)S(1)} %broadcast_bitcast_fusion, bf16[4096,128]{1,0:T(8,128)(2,1)} %param.7), kind=kLoop, calls=%fused_computation.8 | loop fusion | flops 5242880 | bytes 4210688 | tf_op jit(solution)/shard_map/convert_element_type | solution.py:23
  9.6 1.2 broadcast_in_dim.43
  10.8 3.5 %compare_select_fusion = bf16[4096,256]{1,0:T(8,128)(2,1)} fusion(bf16[512,8,2,128]{3,2,1,0:T(2,128)(2,1)S(1)} %bitcast.47, s32[256]{0:T(256)S(1)} %iota_bitcast_fusion, s32[4096]{0:T(1024)S(1)} %broadcast_bitcast_fusion.1), kind=kLoop, calls=%fused_computation.2 | loop fusion | flops 2097152 | bytes 4211712 | tf_op jit(solution)/shard_map/jit(_where)/select_n | solution.py:27
  14.3 0.0 all-gather.3.cloned.1.call-update
  14.3 0.0 all-gather.5.cloned.1.call-start
  14.3 0.7 all-gather.5.cloned.1.call-update
  15.0 0.0 reduce-scatter.2.cloned.1.call-start
  15.1 15.7 %all-gather.3.cloned.1.call-done = bf16[8192,256]{1,0:T(8,128)(2,1)} async-done(((bf16[4096,256]{1,0:T(8,128)(2,1)}), bf16[8192,256]{1,0:T(8,128)(2,1)}) %all-gather.3.cloned.1.call-update) | async-done | bytes 4194320 | tf_op jit(solution)/shard_map/all_gather | solution.py:51
  30.8 128.3 %all-gather.5.cloned.1.call-done = bf16[512,8192]{1,0:T(8,128)(2,1)} async-done(((bf16[512,1024]{1,0:T(8,128)(2,1)}), bf16[512,8192]{1,0:T(8,128)(2,1)}) %all-gather.5.cloned.1.call-update) | async-done | bytes 8388624 | tf_op jit(solution)/shard_map/all_gather | solution.py:47
  159.1 0.0 copy-done.3
  159.1 17.9 %fusion = bf16[8192,256]{0,1:T(8,128)(2,1)} fusion(bf16[512,8192]{1,0:T(8,128)(2,1)} %all-gather.5.cloned.1.call-done, bf16[8192,256]{1,0:T(8,128)(2,1)} %all-gather.3.cloned.1.call-done, bf16[512,256]{1,0:T(8,128)(2,1)S(1)} %copy-done.3), kind=kOutput, calls=%fused_computation.1 | convolution fusion | flops 4297588736 | bytes 17039360 | tf_op jit(solution)/shard_map/dot_general | solution.py:57
  177.0 0.0 reduce-scatter.2.cloned.1.call-update
  177.0 0.6 copy-done.4
  177.6 0.1 bitcast_compare_fusion
  177.7 9.7 %reduce-scatter.2.cloned.1.call-done = bf16[4096,256]{0,1:T(8,128)(2,1)} async-done(((bf16[8192,256]{0,1:T(8,128)(2,1)}), bf16[4096,256]{0,1:T(8,128)(2,1)}) %reduce-scatter.2.cloned.1.call-update) | async-done | bytes 2097168 | tf_op jit(solution)/shard_map/reduce_scatter | solution.py:56
  187.4 3.3 %fusion.7 = (f32[4096,1,1,128]{0,3,2,1:T(8,128)}, f32[4096,1,1,128]{0,3,2,1:T(8,128)S(1)}) fusion(bf16[4096,1,2,128]{0,3,2,1:T(8,128)(2,1)} %bitcast.48), kind=kLoop, calls=%fused_computation.19 | loop fusion | bytes 8388608 | tf_op jit(solution)/shard_map/slice | solution.py:38
  190.7 1.8 copy.10
  192.6 3.0 %copy.9 = f32[4096,1,1,128]{3,0,2,1:T(8,128)} copy(f32[4096,1,1,128]{0,3,2,1:T(8,128)} %get-tuple-element.5) | data formatting | bytes 4194304
  195.6 4.9 %fusion.3 = bf16[4096,128]{1,0:T(8,128)(2,1)} fusion(f32[4096,1,1,128]{3,0,2,1:T(8,128)} %copy.10, f32[4096,1,1,128]{3,0,2,1:T(8,128)} %copy.9, s32[4096,128]{1,0:T(8,128)S(1)} %copy-done.1, pred[4096]{0:T(1024)(128)(4,1)S(1)} %bitcast_compare_fusion, bf16[4096,128]{1,0:T(8,128)(2,1)S(1)} %copy-done.2), kind=kLoop, calls=%fused_computation.6 | loop fusion | flops 6815744 | bytes 8392704 | tf_op jit(solution)/shard_map/convert_element_type | solution.py:64
  (7 shorter events, 0.0 us)
Async XLA Ops:
  6.5 0.7 copy-start
  6.5 24.3 %all-gather.3.cloned.1.call-start = ((), (), s32[]{:S(2)}) async-start(), calls=%async_computation.1 | async-start | bytes 6291456 | tf_op jit(solution)/shard_map/all_gather | solution.py:51
  14.2 144.9 %copy-start.3 = (bf16[512,256]{1,0:T(8,128)(2,1)S(1)}, bf16[512,256]{1,0:T(8,128)(2,1)}, u32[]{:S(2)}) copy-start(bf16[512,256]{1,0:T(8,128)(2,1)} %param.11) | copy-start | bytes 786436
  14.3 144.8 %all-gather.5.cloned.1.call-start = ((), (), s32[]{:S(2)}) async-start(), calls=%async_computation.2 | async-start | bytes 9437184 | tf_op jit(solution)/shard_map/all_gather | solution.py:47
  15.0 172.4 %reduce-scatter.2.cloned.1.call-start = ((), (), s32[]{:S(2)}) async-start(), calls=%async_computation.3 | async-start | bytes 6291456 | tf_op jit(solution)/shard_map/reduce_scatter | solution.py:56
  177.0 0.7 copy-start.4
  192.6 3.0 %copy-start.1 = (s32[4096,128]{1,0:T(8,128)S(1)}, s32[4096,128]{1,0:T(8,128)}, u32[]{:S(2)}) copy-start(s32[4096,128]{1,0:T(8,128)} %param.8) | copy-start | bytes 6291460
  192.6 3.0 %copy-start.2 = (bf16[4096,128]{1,0:T(8,128)(2,1)S(1)}, bf16[4096,128]{1,0:T(8,128)(2,1)}, u32[]{:S(2)}) copy-start(bf16[4096,128]{1,0:T(8,128)(2,1)} %param.7) | copy-start | bytes 3145732
Sparse Core Ops, SparseCore 0:
  14.4 16.3 all-gather.2
  33.0 126.0 all-gather.4
  177.1 10.2 reduce-scatter.1
where the time goes:
time: 207 us
  waiting for transfers between devices  154 us (74%)
  matrix products  17.9 us (9%)
  between operations  13.1 us (6%)
  local copies, waits for them, and re-layouts  10.8 us (5%)
  other arithmetic  10.7 us (5%)
    all_gather x1, waiting for transfers between devices, body(): gathered = lax.all_gather(inputs, 'mp', axis=1, tiled=True)  128 us
    dot_general x1, matrix products, body(): lax.dot_general(columns, resid, (((0,), (0,)), ((), ())), preferred_eleme...  17.9 us
    all_gather x1, waiting for transfers between devices, body(): lax.all_gather(weight, 'dp', axis=0, tiled=True)  15.7 us
    reduce_scatter x1, waiting for transfers between devices, body(): lax.psum_scatter(lax.dot_general(columns, resid, (((0,), (0,)), ((), ()))...  9.67 us
    unnamed x12, local copies, waits for them, and re-layouts  5.51 us
    convert_element_type x1, other arithmetic, body(): return (compact(weight_grad, chosen) * slope).astype(jnp.bfloat16)  4.94 us
  transfers between devices with their start and end apart: 3, of which 3 were waited for; matrix products, arithmetic and copies ran while one was open for 0% of the time, Pallas kernels for 0%

commit v1 on v0

--- a/solution.py
+++ b/solution.py
@@ -3,9 +3,13 @@
 import jax
 import jax.numpy as jnp
 from jax import lax
+from jax.experimental import pallas as pl
+from jax.experimental.pallas import tpu as pltpu
 from jax.sharding import PartitionSpec as P
 
 BLK = 128
+MESH = pl.DeviceIdType.MESH
+NZ, NX = 4, 2
 
 
 def expand_blocks(table, rows, cols):
@@ -64,7 +68,262 @@
     return (compact(weight_grad, chosen) * slope).astype(jnp.bfloat16)
 
 
+def order(step, z):
+    far = z // 2
+    near = z * (1 - far) + (NZ - 1 - z) * far
+    late = step // 2
+    place = (1 - late) * ((step + near) % 2) + late * step
+    return (1 - far) * place + far * (NZ - 1 - place)
+
+
+def kernel(
+    inputs, rounding, codes, scales, pick, target, out,
+    gathered, turned, weight, slope, rounding_v, codes_v, outputs, resid,
+    pick_own, pick_other, scale_rows, outgoing, incoming, kept,
+    local_sem, recv_sem, x_sem, up_sem, down_sem, w_send, w_recv, p_send, p_recv, g_send, g_recv,
+):
+    tokens, features = inputs.shape
+    rows = rounding.shape[0]
+    shards_each = rows // features
+    blocks = features // BLK
+    me = lax.axis_index("mp")
+    dp = lax.axis_index("dp")
+    z, x = me // NX, me % NX
+    other = 1 - dp
+    beside = {"mp": z * NX + (1 - x)}
+    above = {"mp": me + NX}
+    below = {"mp": me - NX}
+    twin = {"dp": other}
+
+    def remote(source, dest, send, recv, device):
+        return pltpu.make_async_remote_copy(
+            src_ref=source, dst_ref=dest, send_sem=send, recv_sem=recv,
+            device_id=device, device_id_type=MESH,
+        )
+
+    own = pltpu.make_async_copy(inputs, gathered.at[me], local_sem.at[0])
+    get_rounding = pltpu.make_async_copy(rounding, rounding_v, local_sem.at[1])
+    get_codes = pltpu.make_async_copy(codes, codes_v, local_sem.at[2])
+    own.start()
+    get_rounding.start()
+    get_codes.start()
+
+    barrier = pltpu.get_barrier_semaphore()
+    pl.semaphore_signal(barrier, inc=1, device_id=beside, device_id_type=MESH)
+    pl.semaphore_signal(barrier, inc=1, device_id=twin, device_id_type=MESH)
+
+    @pl.when(z < NZ - 1)
+    def _():
+        pl.semaphore_signal(barrier, inc=1, device_id=above, device_id_type=MESH)
+
+    @pl.when(z > 0)
+    def _():
+        pl.semaphore_signal(barrier, inc=1, device_id=below, device_id_type=MESH)
+
+    pl.semaphore_wait(barrier, 2 + (z + NZ - 2) // (NZ - 1) + (2 * NZ - 3 - z) // (NZ - 1))
+
+    def sends(step):
+        column = order(step, z)
+        slot = column * NX + x
+        block = gathered.at[slot]
+        arrive = recv_sem.at[slot]
+        return (
+            (column <= z, z < NZ - 1, remote(block, block, up_sem.at[step], arrive, above)),
+            (column >= z, z > 0, remote(block, block, down_sem.at[step], arrive, below)),
+            (True, True, remote(block, block, x_sem.at[step], arrive, beside)),
+        )
+
+    def each_send(step, act):
+        for first, second, copy in sends(step):
+            if first is True:
+                act(copy)
+            else:
+                @pl.when(jnp.logical_and(first, second))
+                def _():
+                    act(copy)
+
+    def arrived(slot):
+        block = gathered.at[slot]
+        remote(block, block, x_sem.at[0], recv_sem.at[slot], beside).wait_recv()
+
+    own.wait()
+    each_send(0, lambda copy: copy.start())
+
+    pick_own[...] = jnp.broadcast_to(pick[...].astype(jnp.float32), pick_own.shape)
+    scale_rows[...] = jnp.broadcast_to(scales[...], scale_rows.shape)
+    send_pick = remote(pick_own, pick_other, p_send, p_recv, twin)
+    send_pick.start()
+    get_rounding.wait()
+    get_codes.wait()
+
+    def soft_block(index, carry):
+        at = pl.ds(pl.multiple_of(index * BLK, BLK), BLK)
+        levels = (codes_v[at, :] - 8).astype(jnp.float32)
+        soft = jax.nn.sigmoid(rounding_v[at, :].astype(jnp.float32))
+        factor = scale_rows[pl.ds(index, 1), :]
+        chosen = pick_own[pl.ds(index, 1), :]
+        value = factor * jnp.clip(levels + soft, -8.0, 7.0)
+        first = jnp.broadcast_to(chosen, value.shape) < 0.5
+        here = pl.ds(pl.multiple_of(dp * rows + index * BLK, BLK), BLK)
+        weight[here, :BLK] = jnp.where(first, value, 0.0).astype(jnp.bfloat16)
+        weight[here, BLK:] = jnp.where(first, 0.0, value).astype(jnp.bfloat16)
+        slope[at, :] = soft * (1.0 - soft) * (levels < 6.5).astype(jnp.float32)
+        return carry
+
+    lax.fori_loop(0, rows // BLK, soft_block, 0)
+    mine = weight.at[pl.ds(pl.multiple_of(dp * rows, BLK), rows), :]
+    send_weight = remote(mine, mine, w_send, w_recv, twin)
+    send_weight.start()
+    outputs[...] = jnp.zeros_like(outputs)
+    send_weight.wait()
+    send_pick.wait()
+
+    width = 2 * BLK
+
+    def add(slot):
+        def part(index, carry):
+            at = pl.ds(pl.multiple_of(index * width, width), width)
+            here = pl.ds(pl.multiple_of(slot * features + index * width, width), width)
+            piece = gathered[slot, :, at]
+            outputs[...] += jnp.dot(piece, weight[here, :], preferred_element_type=jnp.float32)
+            turned[here, :] = piece.T
+            return carry
+
+        lax.fori_loop(0, features // width, part, 0)
+
+    add(me)
+
+    def column_step(step, carry):
+        slot = order(step, z) * NX + x
+        arrived(slot)
+        each_send(step, lambda copy: copy.start())
+        add(slot)
+        return carry
+
+    lax.fori_loop(1, NZ, column_step, 0)
+
+    def beside_step(step, carry):
+        slot = order(step, z) * NX + (1 - x)
+        arrived(slot)
+        add(slot)
+        return carry
+
+    lax.fori_loop(0, NZ, beside_step, 0)
+
+    scale_root = math.sqrt(tokens * 2)
+    resid[...] = ((outputs[...] - target[...].astype(jnp.float32)) / scale_root).astype(jnp.bfloat16)
+
+    def block_grad(start, index, table):
+        here = pl.ds(pl.multiple_of(start + index * width, width), width)
+        full = jnp.dot(turned[here, :], resid[...], preferred_element_type=jnp.float32)
+        parts = []
+        for half in range(2):
+            chosen = table[pl.ds(2 * index + half, 1), :]
+            piece = full[half * BLK:(half + 1) * BLK]
+            first = jnp.broadcast_to(chosen, (BLK, BLK)) < 0.5
+            parts.append(jnp.where(first, piece[:, :BLK], piece[:, BLK:]).astype(jnp.bfloat16))
+        return parts
+
+    steps = features // width
+
+    def grad_send(shard):
+        at = pl.ds(pl.multiple_of(shard * features, features), features)
+        return remote(
+            outgoing.at[at, :], incoming.at[at, :], g_send.at[shard], g_recv.at[shard], twin
+        )
+
+    def send_shard(shard, carry):
+        def part(index, carry):
+            index = shard * steps + index
+            first, second = block_grad(other * rows, index, pick_other)
+            outgoing[pl.ds(pl.multiple_of(index * width, width), BLK), :] = first
+            outgoing[pl.ds(pl.multiple_of(index * width + BLK, BLK), BLK), :] = second
+            return carry
+
+        lax.fori_loop(0, steps, part, 0)
+        grad_send(shard).start()
+        return carry
+
+    lax.fori_loop(0, shards_each, send_shard, 0)
+
+    def keep_shard(index, carry):
+        first, second = block_grad(dp * rows, index, pick_own)
+        kept[pl.ds(pl.multiple_of(index * width, width), BLK), :] = first
+        kept[pl.ds(pl.multiple_of(index * width + BLK, BLK), BLK), :] = second
+        return carry
+
+    lax.fori_loop(0, shards_each * steps, keep_shard, 0)
+
+    def finish(shard, carry):
+        grad_send(shard).wait()
+
+        def part(index, carry):
+            at = pl.ds(pl.multiple_of(shard * features + index * BLK, BLK), BLK)
+            total = kept[at, :].astype(jnp.float32) + incoming[at, :].astype(jnp.float32)
+            out[at, :] = (total * slope[at, :]).astype(jnp.bfloat16)
+            return carry
+
+        return lax.fori_loop(0, blocks, part, carry)
+
+    lax.fori_loop(0, shards_each, finish, 0)
+
+    def drain(step, carry):
+        each_send(step, lambda copy: copy.wait_send())
+        return carry
+
+    lax.fori_loop(0, NZ, drain, 0)
+
+
+def fused(inputs, rounding, codes, scales, pick, target):
+    tokens, features = inputs.shape
+    rows = rounding.shape[0]
+    shards = NZ * NX
+    every = shards * features
+    anywhere = pl.BlockSpec(memory_space=pl.ANY)
+    near = pl.BlockSpec(memory_space=pltpu.VMEM)
+    bf16, f32 = jnp.bfloat16, jnp.float32
+    dma = pltpu.SemaphoreType.DMA
+    return pl.pallas_call(
+        kernel,
+        out_shape=jax.ShapeDtypeStruct((rows, BLK), bf16),
+        in_specs=[anywhere, anywhere, anywhere, near, near, near],
+        out_specs=near,
+        scratch_shapes=[
+            pltpu.VMEM((shards, tokens, features), bf16),
+            pltpu.VMEM((every, tokens), bf16),
+            pltpu.VMEM((every, 2 * BLK), bf16),
+            pltpu.VMEM((rows, BLK), f32),
+            pltpu.VMEM((rows, BLK), bf16),
+            pltpu.VMEM((rows, BLK), jnp.int32),
+            pltpu.VMEM((tokens, 2 * BLK), f32),
+            pltpu.VMEM((tokens, 2 * BLK), bf16),
+            pltpu.VMEM((rows // BLK, BLK), f32),
+            pltpu.VMEM((rows // BLK, BLK), f32),
+            pltpu.VMEM((rows // BLK, BLK), f32),
+            pltpu.VMEM((rows, BLK), bf16),
+            pltpu.VMEM((rows, BLK), bf16),
+            pltpu.VMEM((rows, BLK), bf16),
+            dma((3,)),
+            dma((shards,)),
+            dma((NZ,)),
+            dma((NZ,)),
+            dma((NZ,)),
+            dma(()),
+            dma(()),
+            dma(()),
+            dma(()),
+            dma((rows // features,)),
+            dma((rows // features,)),
+        ],
+        compiler_params=pltpu.CompilerParams(
+            collective_id=0, has_side_effects=True, vmem_limit_bytes=50 * 1024 * 1024
+        ),
+    )(inputs, rounding, codes, scales, pick, target)
+
+
 def solution(mesh):
+    grid = mesh.shape["mp"] == NZ * NX and mesh.shape["dp"] == 2
+    run = fused if grid else body
     in_specs = (
         P(("groups", "dp"), "mp"),
         P(("groups", "dp"), "mp"),
@@ -74,4 +333,4 @@
         P(("groups", "dp"), "mp"),
     )
     out_specs = P(("groups", "dp"), "mp")
-    return jax.shard_map(body, mesh=mesh, in_specs=in_specs, out_specs=out_specs, check_vma=False)
+    return jax.shard_map(run, mesh=mesh, in_specs=in_specs, out_specs=out_specs, check_vma=False)

time: 207 us -> 114 us (0.55)
  waiting for transfers between devices: 154 us -> 0 us
  Pallas kernels: 0 us -> 107 us
  matrix products: 17.9 us -> 0 us
  between operations: 13.1 us -> 0.01 us
  other arithmetic: 10.7 us -> 0 us
  local copies, waits for them, and re-layouts: 10.8 us -> 5.84 us
    all_gather x2 -> x0, waiting for transfers between devices: 144 us -> none  [the longest x1 128 us: body(): gathered = lax.all_gather(inputs, 'mp', axis=1, tiled=True)]
    pallas_call x0 -> x1, Pallas kernels: none -> 107 us  [fused(): pl.pallas_call(kernel, out_shape=jax.ShapeDtypeStruct((rows, BLK), bf16),...]
    dot_general x1 -> x0, matrix products: 17.9 us -> none  [body(): lax.dot_general(columns, resid, (((0,), (0,)), ((), ())), preferred_eleme...]
    reduce_scatter x1 -> x0, waiting for transfers between devices: 9.67 us -> none  [body(): lax.psum_scatter(lax.dot_general(columns, resid, (((0,), (0,)), ((), ()))...]
    convert_element_type x2 -> x0, other arithmetic: 7.18 us -> none  [the longest x1 4.94 us: body(): return (compact(weight_grad, chosen) * slope).astype(jnp.bfloat16)]
    select_n x1 -> x0, other arithmetic: 3.48 us -> none  [soft_weights(): jnp.where(chosen == places, spread, jnp.zeros((), jnp.bfloat16))]
    slice x1 -> x0, local copies, waits for them, and re-layouts: 3.35 us -> none  [compact(): pieces[:, :, 0, :]]
    unnamed x12 -> x9, local copies, waits for them, and re-layouts: 5.51 us -> 5.84 us
  transfers between devices with their start and end apart: 3 -> 0, of which waited for: 3 -> 0; matrix products, arithmetic and copies ran while one was open for 0% -> 0% of each run, Pallas kernels for 0% -> 0%
where the time goes in v1:
time: 114 us; the launch traced here: 113 us
  Pallas kernels  107 us (94%)
  local copies, waits for them, and re-layouts  5.84 us (5%)
    pallas_call x1, Pallas kernels, fused(): pl.pallas_call(kernel, out_shape=jax.ShapeDtypeStruct((rows, BLK), bf16),...  107 us
    unnamed x9, local copies, waits for them, and re-layouts  5.84 us

profile of v1, /device:TPU:0, one launch (start us, length us, event | category | flops | bytes accessed | tf_op | source)
XLA Modules:
  0.0 113.3 jit_solution(12352913017777121971)
XLA Ops:
  0.0 0.7 copy.7.scales
  0.7 0.7 copy.8.pick
  1.5 0.0 copy-start
  1.5 1.2 %copy-done = bf16[512,1024]{1,0:T(8,128)(2,1)S(1)} copy-done((bf16[512,1024]{1,0:T(8,128)(2,1)S(1)}, bf16[512,1024]{1,0:T(8,128)(2,1)}, u32[]{:S(2)}) %copy-start) | copy-done | bytes 1048600
  2.7 0.0 copy-start.1
  2.7 1.2 %copy-done.1 = bf16[4096,128]{1,0:T(8,128)(2,1)S(1)} copy-done((bf16[4096,128]{1,0:T(8,128)(2,1)S(1)}, bf16[4096,128]{1,0:T(8,128)(2,1)}, u32[]{:S(2)}) %copy-start.1) | copy-done | bytes 1048600
  3.9 0.0 copy-start.2
  3.9 0.9 copy-done.2
  4.9 107.5 %shard_map.64 = bf16[4096,128]{1,0:T(8,128)(2,1)S(1)} custom-call(bf16[512,1024]{1,0:T(8,128)(2,1)S(1)} %copy-done, bf16[4096,128]{1,0:T(8,128)(2,1)S(1)} %copy-done.1, s32[4096,128]{1,0:T(8,128)} %codes.1, f32[32,1]{1,0:T(8,128)S(1)} %copy.7.scales, s32[32,1]{1,0:T(8,128)S(1)} %copy.8.pick, bf16[512,256]{1,0:T(8,128)(2,1)S(1)} %copy-done.2), custom_call_target="tpu_custom_call" | custom-call | tf_op jit(solution)/shard_map/pallas_call | solution.py:286
  112.3 1.0 copy.10
Async XLA Ops:
  1.5 1.2 %copy-start = (bf16[512,1024]{1,0:T(8,128)(2,1)S(1)}, bf16[512,1024]{1,0:T(8,128)(2,1)}, u32[]{:S(2)}) copy-start(bf16[512,1024]{1,0:T(8,128)(2,1)} %inputs.1) | copy-start | bytes 3145732
  2.7 1.2 %copy-start.1 = (bf16[4096,128]{1,0:T(8,128)(2,1)S(1)}, bf16[4096,128]{1,0:T(8,128)(2,1)}, u32[]{:S(2)}) copy-start(bf16[4096,128]{1,0:T(8,128)(2,1)} %rounding.1) | copy-start | bytes 3145732
  3.9 0.9 copy-start.2

commit v2 on v1

--- a/solution.py
+++ b/solution.py
@@ -122,32 +122,45 @@
 
     pl.semaphore_wait(barrier, 2 + (z + NZ - 2) // (NZ - 1) + (2 * NZ - 3 - z) // (NZ - 1))
 
-    def sends(step):
+    lead = tokens * 5 // 512 * 16
+    middle = lead + (tokens - lead + 16) // 32 * 16
+    bounds = ((lead, middle), (middle, tokens), (0, lead))
+
+    def piece_copies(step, side, piece):
         column = order(step, z)
-        slot = column * NX + x
-        block = gathered.at[slot]
-        arrive = recv_sem.at[slot]
+        slot = column * NX + (x if side == 0 else 1 - x)
+        start, stop = bounds[piece]
+        block = gathered.at[slot, pl.ds(start, stop - start), :]
+        arrive = recv_sem.at[slot, piece]
+        lane = piece + side
         return (
-            (column <= z, z < NZ - 1, remote(block, block, up_sem.at[step], arrive, above)),
-            (column >= z, z > 0, remote(block, block, down_sem.at[step], arrive, below)),
-            (True, True, remote(block, block, x_sem.at[step], arrive, beside)),
+            (column <= z, z < NZ - 1, lambda: remote(block, block, up_sem.at[step, lane], arrive, above)),
+            (column >= z, z > 0, lambda: remote(block, block, down_sem.at[step, lane], arrive, below)),
+            lambda: remote(block, block, x_sem.at[step, piece], arrive, beside),
         )
 
-    def each_send(step, act):
-        for first, second, copy in sends(step):
-            if first is True:
-                act(copy)
-            else:
-                @pl.when(jnp.logical_and(first, second))
-                def _():
-                    act(copy)
-
-    def arrived(slot):
-        block = gathered.at[slot]
-        remote(block, block, x_sem.at[0], recv_sem.at[slot], beside).wait_recv()
+    def along(step, side, piece, act):
+        for first, second, copy in piece_copies(step, side, piece)[:2]:
+
+            @pl.when(jnp.logical_and(first, second))
+            def _():
+                act(copy())
+
+    def across(step, piece, act):
+        act(piece_copies(step, 0, piece)[2]())
+
+    def arrived(step, side, piece):
+        piece_copies(step, side, piece)[2]().wait_recv()
+
+    def begin(copy):
+        copy.start()
 
     own.wait()
-    each_send(0, lambda copy: copy.start())
+    across(0, 2, begin)
+    for piece in range(3):
+        along(0, 0, piece, begin)
+        if piece < 2:
+            across(0, piece, begin)
 
     pick_own[...] = jnp.broadcast_to(pick[...].astype(jnp.float32), pick_own.shape)
     scale_rows[...] = jnp.broadcast_to(scales[...], scale_rows.shape)
@@ -174,6 +187,8 @@
     mine = weight.at[pl.ds(pl.multiple_of(dp * rows, BLK), rows), :]
     send_weight = remote(mine, mine, w_send, w_recv, twin)
     send_weight.start()
+    arrived(0, 1, 2)
+    along(0, 1, 2, begin)
     outputs[...] = jnp.zeros_like(outputs)
     send_weight.wait()
     send_pick.wait()
@@ -194,21 +209,29 @@
     add(me)
 
     def column_step(step, carry):
-        slot = order(step, z) * NX + x
-        arrived(slot)
-        each_send(step, lambda copy: copy.start())
-        add(slot)
+        for piece in range(2):
+            arrived(step, 0, piece)
+            along(step, 0, piece, begin)
+            across(step, piece, begin)
         return carry
 
     lax.fori_loop(1, NZ, column_step, 0)
-
-    def beside_step(step, carry):
-        slot = order(step, z) * NX + (1 - x)
-        arrived(slot)
-        add(slot)
-        return carry
-
-    lax.fori_loop(0, NZ, beside_step, 0)
+    for piece in range(2):
+        arrived(0, 1, piece)
+    add(z * NX + 1 - x)
+
+    def lead_step(step, carry):
+        for side in range(2):
+            arrived(step, side, 2)
+            along(step, side, 2, begin)
+        column = order(step, z)
+        add(column * NX + x)
+        for piece in range(2):
+            arrived(step, 1, piece)
+        add(column * NX + 1 - x)
+        return carry
+
+    lax.fori_loop(1, NZ, lead_step, 0)
 
     scale_root = math.sqrt(tokens * 2)
     resid[...] = ((outputs[...] - target[...].astype(jnp.float32)) / scale_root).astype(jnp.bfloat16)
@@ -267,10 +290,18 @@
 
     lax.fori_loop(0, shards_each, finish, 0)
 
+    def finished(copy):
+        copy.wait_send()
+
     def drain(step, carry):
-        each_send(step, lambda copy: copy.wait_send())
-        return carry
-
+        for piece in range(3):
+            along(step, 0, piece, finished)
+        along(step, 1, 2, finished)
+        for piece in range(2):
+            across(step, piece, finished)
+        return carry
+
+    across(0, 2, finished)
     lax.fori_loop(0, NZ, drain, 0)
 
 
@@ -304,10 +335,10 @@
             pltpu.VMEM((rows, BLK), bf16),
             pltpu.VMEM((rows, BLK), bf16),
             dma((3,)),
-            dma((shards,)),
-            dma((NZ,)),
-            dma((NZ,)),
-            dma((NZ,)),
+            dma((shards, 3)),
+            dma((NZ, 3)),
+            dma((NZ, 4)),
+            dma((NZ, 4)),
             dma(()),
             dma(()),
             dma(()),
@@ -316,7 +347,7 @@
             dma((rows // features,)),
         ],
         compiler_params=pltpu.CompilerParams(
-            collective_id=0, has_side_effects=True, vmem_limit_bytes=50 * 1024 * 1024
+            collective_id=0, has_side_effects=True, vmem_limit_bytes=60 * 1024 * 1024
         ),
     )(inputs, rounding, codes, scales, pick, target)
 

time: 114 us -> 101 us (0.89)
  Pallas kernels: 107 us -> 96.1 us
    pallas_call x1, Pallas kernels: 107 us -> 96.1 us  [fused(): pl.pallas_call(kernel, out_shape=jax.ShapeDtypeStruct((rows, BLK), bf16),...]
    unnamed x9 -> x3, local copies, waits for them, and re-layouts: 5.84 us -> 4.94 us
where the time goes in v2:
time: 101 us
  Pallas kernels  96.1 us (95%)
  local copies, waits for them, and re-layouts  4.94 us (5%)
    pallas_call x1, Pallas kernels, fused(): pl.pallas_call(kernel, out_shape=jax.ShapeDtypeStruct((rows, BLK), bf16),...  96.1 us
    unnamed x3, local copies, waits for them, and re-layouts  4.94 us

profile of v2, /device:TPU:0, one launch (start us, length us, event | category | flops | bytes accessed | tf_op | source)
XLA Modules:
  0.0 101.0 jit_solution(2228641516349110582)
XLA Ops:
  0.0 1.3 %copy.7.scales = f32[32,1]{1,0:T(8,128)} copy(f32[32,1]{0,1:T(1,128)} %param.9) | data formatting | bytes 256 | tf_op args[3]
  1.3 1.3 %copy.8.pick = s32[32,1]{1,0:T(8,128)} copy(s32[32,1]{0,1:T(1,128)} %param.10) | data formatting | bytes 256 | tf_op args[4]
  2.7 96.1 %shard_map.64 = bf16[4096,128]{1,0:T(8,128)(2,1)} custom-call(bf16[512,1024]{1,0:T(8,128)(2,1)} %inputs.1, bf16[4096,128]{1,0:T(8,128)(2,1)} %rounding.1, s32[4096,128]{1,0:T(8,128)} %codes.1, f32[32,1]{1,0:T(8,128)} %copy.7.scales, s32[32,1]{1,0:T(8,128)} %copy.8.pick, bf16[512,256]{1,0:T(8,128)(2,1)} %target.1), custom_call_target="tpu_custom_call" | custom-call | tf_op jit(solution)/shard_map/pallas_call | solution.py:317
  98.7 2.3 %copy.10 = bf16[4096,128]{1,0:T(8,128)(2,1)} copy(bf16[4096,128]{1,0:T(8,128)(2,1)} %shard_map.64) | data formatting | bytes 2097152

commit v3 on v2

--- a/solution.py
+++ b/solution.py
@@ -79,8 +79,8 @@
 def kernel(
     inputs, rounding, codes, scales, pick, target, out,
     gathered, turned, weight, slope, rounding_v, codes_v, outputs, resid,
-    pick_own, pick_other, scale_rows, outgoing, incoming, kept,
-    local_sem, recv_sem, x_sem, up_sem, down_sem, w_send, w_recv, p_send, p_recv, g_send, g_recv,
+    pick_own, scale_rows, turned_other, resid_other, kept,
+    local_sem, recv_sem, x_sem, up_sem, down_sem, w_send, w_recv, r_send, r_recv, t_send, t_recv,
 ):
     tokens, features = inputs.shape
     rows = rounding.shape[0]
@@ -126,28 +126,29 @@
     middle = lead + (tokens - lead + 16) // 32 * 16
     bounds = ((lead, middle), (middle, tokens), (0, lead))
 
-    def piece_copies(step, side, piece):
+    def piece_copies(step, side, piece, fresh=False):
         column = order(step, z)
         slot = column * NX + (x if side == 0 else 1 - x)
         start, stop = bounds[piece]
         block = gathered.at[slot, pl.ds(start, stop - start), :]
+        source = inputs.at[pl.ds(start, stop - start), :] if fresh else block
         arrive = recv_sem.at[slot, piece]
         lane = piece + side
         return (
-            (column <= z, z < NZ - 1, lambda: remote(block, block, up_sem.at[step, lane], arrive, above)),
-            (column >= z, z > 0, lambda: remote(block, block, down_sem.at[step, lane], arrive, below)),
-            lambda: remote(block, block, x_sem.at[step, piece], arrive, beside),
+            (column <= z, z < NZ - 1, lambda: remote(source, block, up_sem.at[step, lane], arrive, above)),
+            (column >= z, z > 0, lambda: remote(source, block, down_sem.at[step, lane], arrive, below)),
+            lambda: remote(source, block, x_sem.at[step, piece], arrive, beside),
         )
 
-    def along(step, side, piece, act):
-        for first, second, copy in piece_copies(step, side, piece)[:2]:
+    def along(step, side, piece, act, fresh=False):
+        for first, second, copy in piece_copies(step, side, piece, fresh)[:2]:
 
             @pl.when(jnp.logical_and(first, second))
             def _():
                 act(copy())
 
-    def across(step, piece, act):
-        act(piece_copies(step, 0, piece)[2]())
+    def across(step, piece, act, fresh=False):
+        act(piece_copies(step, 0, piece, fresh)[2]())
 
     def arrived(step, side, piece):
         piece_copies(step, side, piece)[2]().wait_recv()
@@ -155,17 +156,15 @@
     def begin(copy):
         copy.start()
 
-    own.wait()
-    across(0, 2, begin)
+    across(0, 2, begin, True)
     for piece in range(3):
-        along(0, 0, piece, begin)
+        along(0, 0, piece, begin, True)
         if piece < 2:
-            across(0, piece, begin)
-
-    pick_own[...] = jnp.broadcast_to(pick[...].astype(jnp.float32), pick_own.shape)
-    scale_rows[...] = jnp.broadcast_to(scales[...], scale_rows.shape)
-    send_pick = remote(pick_own, pick_other, p_send, p_recv, twin)
-    send_pick.start()
+            across(0, piece, begin, True)
+
+    across_lanes = (BLK, rows // BLK)
+    pick_own[...] = jnp.broadcast_to(pick[...].astype(jnp.float32), across_lanes).T
+    scale_rows[...] = jnp.broadcast_to(scales[...], across_lanes).T
     get_rounding.wait()
     get_codes.wait()
 
@@ -191,9 +190,17 @@
     along(0, 1, 2, begin)
     outputs[...] = jnp.zeros_like(outputs)
     send_weight.wait()
-    send_pick.wait()
 
     width = 2 * BLK
+    steps = features // width
+
+    def turned_copy(slot):
+        place = slot % shards_each
+        return remote(
+            turned.at[pl.ds(pl.multiple_of(slot * features, features), features), :],
+            turned_other.at[pl.ds(pl.multiple_of(place * features, features), features), :],
+            t_send.at[place], t_recv.at[place], twin,
+        )
 
     def add(slot):
         def part(index, carry):
@@ -204,8 +211,13 @@
             turned[here, :] = piece.T
             return carry
 
-        lax.fori_loop(0, features // width, part, 0)
-
+        lax.fori_loop(0, steps, part, 0)
+
+        @pl.when(slot // shards_each == other)
+        def _():
+            turned_copy(slot).start()
+
+    own.wait()
     add(me)
 
     def column_step(step, carry):
@@ -236,59 +248,50 @@
     scale_root = math.sqrt(tokens * 2)
     resid[...] = ((outputs[...] - target[...].astype(jnp.float32)) / scale_root).astype(jnp.bfloat16)
 
-    def block_grad(start, index, table):
+    send_resid = remote(resid, resid_other, r_send, r_recv, twin)
+    send_resid.start()
+
+    def block_grad(rows_of, start, index, errors):
         here = pl.ds(pl.multiple_of(start + index * width, width), width)
-        full = jnp.dot(turned[here, :], resid[...], preferred_element_type=jnp.float32)
+        full = jnp.dot(rows_of[here, :], errors[...], preferred_element_type=jnp.float32)
         parts = []
         for half in range(2):
-            chosen = table[pl.ds(2 * index + half, 1), :]
+            chosen = pick_own[pl.ds(2 * index + half, 1), :]
             piece = full[half * BLK:(half + 1) * BLK]
             first = jnp.broadcast_to(chosen, (BLK, BLK)) < 0.5
             parts.append(jnp.where(first, piece[:, :BLK], piece[:, BLK:]).astype(jnp.bfloat16))
         return parts
 
-    steps = features // width
-
-    def grad_send(shard):
-        at = pl.ds(pl.multiple_of(shard * features, features), features)
-        return remote(
-            outgoing.at[at, :], incoming.at[at, :], g_send.at[shard], g_recv.at[shard], twin
-        )
-
-    def send_shard(shard, carry):
+    def keep(index, carry):
+        for half, term in enumerate(block_grad(turned, dp * rows, index, resid)):
+            kept[pl.ds(pl.multiple_of(index * width + half * BLK, BLK), BLK), :] = term
+        return carry
+
+    lax.fori_loop(0, shards_each * steps, keep, 0)
+    send_resid.wait()
+
+    def finish(turn, carry):
+        far = z // 2
+        place = (1 - far) * turn + far * (shards_each - 1 - turn)
+        turned_copy(dp * shards_each + place).wait_recv()
+
         def part(index, carry):
-            index = shard * steps + index
-            first, second = block_grad(other * rows, index, pick_other)
-            outgoing[pl.ds(pl.multiple_of(index * width, width), BLK), :] = first
-            outgoing[pl.ds(pl.multiple_of(index * width + BLK, BLK), BLK), :] = second
+            index = place * steps + index
+            for half, term in enumerate(block_grad(turned_other, 0, index, resid_other)):
+                at = pl.ds(pl.multiple_of(index * width + half * BLK, BLK), BLK)
+                total = kept[at, :].astype(jnp.float32) + term.astype(jnp.float32)
+                out[at, :] = (total * slope[at, :]).astype(jnp.bfloat16)
             return carry
 
-        lax.fori_loop(0, steps, part, 0)
-        grad_send(shard).start()
-        return carry
-
-    lax.fori_loop(0, shards_each, send_shard, 0)
-
-    def keep_shard(index, carry):
-        first, second = block_grad(dp * rows, index, pick_own)
-        kept[pl.ds(pl.multiple_of(index * width, width), BLK), :] = first
-        kept[pl.ds(pl.multiple_of(index * width + BLK, BLK), BLK), :] = second
-        return carry
-
-    lax.fori_loop(0, shards_each * steps, keep_shard, 0)
-
-    def finish(shard, carry):
-        grad_send(shard).wait()
-
-        def part(index, carry):
-            at = pl.ds(pl.multiple_of(shard * features + index * BLK, BLK), BLK)
-            total = kept[at, :].astype(jnp.float32) + incoming[at, :].astype(jnp.float32)
-            out[at, :] = (total * slope[at, :]).astype(jnp.bfloat16)
-            return carry
-
-        return lax.fori_loop(0, blocks, part, carry)
+        return lax.fori_loop(0, steps, part, carry)
 
     lax.fori_loop(0, shards_each, finish, 0)
+
+    def sent(place, carry):
+        turned_copy(other * shards_each + place).wait_send()
+        return carry
+
+    lax.fori_loop(0, shards_each, sent, 0)
 
     def finished(copy):
         copy.wait_send()
@@ -310,7 +313,7 @@
     rows = rounding.shape[0]
     shards = NZ * NX
     every = shards * features
-    anywhere = pl.BlockSpec(memory_space=pl.ANY)
+    anywhere = pl.BlockSpec(memory_space=pltpu.HBM)
     near = pl.BlockSpec(memory_space=pltpu.VMEM)
     bf16, f32 = jnp.bfloat16, jnp.float32
     dma = pltpu.SemaphoreType.DMA
@@ -330,9 +333,8 @@
             pltpu.VMEM((tokens, 2 * BLK), bf16),
             pltpu.VMEM((rows // BLK, BLK), f32),
             pltpu.VMEM((rows // BLK, BLK), f32),
-            pltpu.VMEM((rows // BLK, BLK), f32),
-            pltpu.VMEM((rows, BLK), bf16),
-            pltpu.VMEM((rows, BLK), bf16),
+            pltpu.VMEM((rows, tokens), bf16),
+            pltpu.VMEM((tokens, 2 * BLK), bf16),
             pltpu.VMEM((rows, BLK), bf16),
             dma((3,)),
             dma((shards, 3)),
@@ -349,7 +351,7 @@
         compiler_params=pltpu.CompilerParams(
             collective_id=0, has_side_effects=True, vmem_limit_bytes=60 * 1024 * 1024
         ),
-    )(inputs, rounding, codes, scales, pick, target)
+    )(inputs, rounding, codes, scales.T, pick.T, target)
 
 
 def solution(mesh):

time: 101 us -> 98.3 us (0.973)
  local copies, waits for them, and re-layouts: 4.94 us -> 2.26 us
    unnamed x3 -> x1, local copies, waits for them, and re-layouts: 4.94 us -> 2.26 us
where the time goes in v3:
time: 98.3 us; the launch traced here: 98.2 us
  Pallas kernels  95.9 us (98%)
  local copies, waits for them, and re-layouts  2.26 us (2%)
    pallas_call x1, Pallas kernels, fused(): pl.pallas_call(kernel, out_shape=jax.ShapeDtypeStruct((rows, BLK), bf16),...  95.9 us
    unnamed x1, local copies, waits for them, and re-layouts  2.26 us

profile of v3, /device:TPU:0, one launch (start us, length us, event | category | flops | bytes accessed | tf_op | source)
XLA Modules:
  0.0 98.2 jit_solution(4637982984113493593)
XLA Ops:
  0.0 95.9 %shard_map.64 = bf16[4096,128]{1,0:T(8,128)(2,1)} custom-call(bf16[512,1024]{1,0:T(8,128)(2,1)} %inputs.1, bf16[4096,128]{1,0:T(8,128)(2,1)} %rounding.1, s32[4096,128]{1,0:T(8,128)} %codes.1, f32[1,32]{1,0:T(1,128)} %bitcast.2, s32[1,32]{1,0:T(1,128)} %bitcast.3, bf16[512,256]{1,0:T(8,128)(2,1)} %target.1), custom_call_target="tpu_custom_call" | custom-call | tf_op jit(solution)/shard_map/pallas_call | solution.py:320
  95.9 2.3 %copy.8 = bf16[4096,128]{1,0:T(8,128)(2,1)} copy(bf16[4096,128]{1,0:T(8,128)(2,1)} %shard_map.64) | data formatting | bytes 2097152

commit v4 on v3

--- a/solution.py
+++ b/solution.py
@@ -79,8 +79,8 @@
 def kernel(
     inputs, rounding, codes, scales, pick, target, out,
     gathered, turned, weight, slope, rounding_v, codes_v, outputs, resid,
-    pick_own, scale_rows, turned_other, resid_other, kept,
-    local_sem, recv_sem, x_sem, up_sem, down_sem, w_send, w_recv, r_send, r_recv, t_send, t_recv,
+    pick_own, scale_rows, turned_other, resid_other, kept, result,
+    local_sem, recv_sem, x_sem, up_sem, down_sem, w_send, w_recv, r_send, r_recv, t_send, t_recv, out_sem,
 ):
     tokens, features = inputs.shape
     rows = rounding.shape[0]
@@ -211,7 +211,7 @@
             turned[here, :] = piece.T
             return carry
 
-        lax.fori_loop(0, steps, part, 0)
+        lax.fori_loop(0, steps, part, 0, unroll=4)
 
         @pl.when(slot // shards_each == other)
         def _():
@@ -267,7 +267,7 @@
             kept[pl.ds(pl.multiple_of(index * width + half * BLK, BLK), BLK), :] = term
         return carry
 
-    lax.fori_loop(0, shards_each * steps, keep, 0)
+    lax.fori_loop(0, shards_each * steps, keep, 0, unroll=4)
     send_resid.wait()
 
     def finish(turn, carry):
@@ -280,15 +280,22 @@
             for half, term in enumerate(block_grad(turned_other, 0, index, resid_other)):
                 at = pl.ds(pl.multiple_of(index * width + half * BLK, BLK), BLK)
                 total = kept[at, :].astype(jnp.float32) + term.astype(jnp.float32)
-                out[at, :] = (total * slope[at, :]).astype(jnp.bfloat16)
+                result[at, :] = (total * slope[at, :]).astype(jnp.bfloat16)
             return carry
 
-        return lax.fori_loop(0, steps, part, carry)
+        lax.fori_loop(0, steps, part, 0, unroll=4)
+        put(place).start()
+        return carry
+
+    def put(place):
+        at = pl.ds(pl.multiple_of(place * features, features), features)
+        return pltpu.make_async_copy(result.at[at, :], out.at[at, :], out_sem.at[place])
 
     lax.fori_loop(0, shards_each, finish, 0)
 
     def sent(place, carry):
         turned_copy(other * shards_each + place).wait_send()
+        put(place).wait()
         return carry
 
     lax.fori_loop(0, shards_each, sent, 0)
@@ -321,7 +328,7 @@
         kernel,
         out_shape=jax.ShapeDtypeStruct((rows, BLK), bf16),
         in_specs=[anywhere, anywhere, anywhere, near, near, near],
-        out_specs=near,
+        out_specs=anywhere,
         scratch_shapes=[
             pltpu.VMEM((shards, tokens, features), bf16),
             pltpu.VMEM((every, tokens), bf16),
@@ -336,6 +343,7 @@
             pltpu.VMEM((rows, tokens), bf16),
             pltpu.VMEM((tokens, 2 * BLK), bf16),
             pltpu.VMEM((rows, BLK), bf16),
+            pltpu.VMEM((rows, BLK), bf16),
             dma((3,)),
             dma((shards, 3)),
             dma((NZ, 3)),
@@ -347,6 +355,7 @@
             dma(()),
             dma((rows // features,)),
             dma((rows // features,)),
+            dma((rows // features,)),
         ],
         compiler_params=pltpu.CompilerParams(
             collective_id=0, has_side_effects=True, vmem_limit_bytes=60 * 1024 * 1024

time: 98.3 us -> 94.8 us (0.964)
  Pallas kernels: 95.9 us -> 92.4 us
    pallas_call x1, Pallas kernels: 95.9 us -> 92.4 us  [fused(): pl.pallas_call(kernel, out_shape=jax.ShapeDtypeStruct((rows, BLK), bf16),...]
where the time goes in v4:
time: 94.8 us; the launch traced here: 94.7 us
  Pallas kernels  92.4 us (97%)
  local copies, waits for them, and re-layouts  2.26 us (2%)
    pallas_call x1, Pallas kernels, fused(): pl.pallas_call(kernel, out_shape=jax.ShapeDtypeStruct((rows, BLK), bf16),...  92.4 us
    unnamed x1, local copies, waits for them, and re-layouts  2.26 us

profile of v4, /device:TPU:0, one launch (start us, length us, event | category | flops | bytes accessed | tf_op | source)
XLA Modules:
  0.0 94.7 jit_solution(20585735512604268)
XLA Ops:
  0.0 92.4 %shard_map.64 = bf16[4096,128]{1,0:T(8,128)(2,1)} custom-call(bf16[512,1024]{1,0:T(8,128)(2,1)} %inputs.1, bf16[4096,128]{1,0:T(8,128)(2,1)} %rounding.1, s32[4096,128]{1,0:T(8,128)} %codes.1, f32[1,32]{1,0:T(1,128)} %bitcast.2, s32[1,32]{1,0:T(1,128)} %bitcast.3, bf16[512,256]{1,0:T(8,128)(2,1)} %target.1), custom_call_target="tpu_custom_call" | custom-call | tf_op jit(solution)/shard_map/pallas_call | solution.py:327
  92.4 2.3 %copy.8 = bf16[4096,128]{1,0:T(8,128)(2,1)} copy(bf16[4096,128]{1,0:T(8,128)(2,1)} %shard_map.64) | data formatting | bytes 2097152

commit v5 on v4

--- a/solution.py
+++ b/solution.py
@@ -123,7 +123,7 @@
     pl.semaphore_wait(barrier, 2 + (z + NZ - 2) // (NZ - 1) + (2 * NZ - 3 - z) // (NZ - 1))
 
     lead = tokens * 5 // 512 * 16
-    middle = lead + (tokens - lead + 16) // 32 * 16
+    middle = tokens // 2
     bounds = ((lead, middle), (middle, tokens), (0, lead))
 
     def piece_copies(step, side, piece, fresh=False):
@@ -194,28 +194,35 @@
     width = 2 * BLK
     steps = features // width
 
-    def turned_copy(slot):
+    def turned_copy(slot, half):
         place = slot % shards_each
+        side = pl.ds(half * middle, middle)
         return remote(
-            turned.at[pl.ds(pl.multiple_of(slot * features, features), features), :],
-            turned_other.at[pl.ds(pl.multiple_of(place * features, features), features), :],
-            t_send.at[place], t_recv.at[place], twin,
+            turned.at[pl.ds(pl.multiple_of(slot * features, features), features), side],
+            turned_other.at[pl.ds(pl.multiple_of(place * features, features), features), side],
+            t_send.at[place, half], t_recv.at[place, half], twin,
         )
 
-    def add(slot):
+    def add_half(slot, half):
+        some = pl.ds(half * middle, middle)
+
         def part(index, carry):
             at = pl.ds(pl.multiple_of(index * width, width), width)
             here = pl.ds(pl.multiple_of(slot * features + index * width, width), width)
-            piece = gathered[slot, :, at]
-            outputs[...] += jnp.dot(piece, weight[here, :], preferred_element_type=jnp.float32)
-            turned[here, :] = piece.T
+            piece = gathered[slot, some, at]
+            outputs[some, :] += jnp.dot(piece, weight[here, :], preferred_element_type=jnp.float32)
+            turned[here, some] = piece.T
             return carry
 
         lax.fori_loop(0, steps, part, 0, unroll=4)
 
         @pl.when(slot // shards_each == other)
         def _():
-            turned_copy(slot).start()
+            turned_copy(slot, half).start()
+
+    def add(slot):
+        add_half(slot, 0)
+        add_half(slot, 1)
 
     own.wait()
     add(me)
@@ -240,7 +247,7 @@
         add(column * NX + x)
         for piece in range(2):
             arrived(step, 1, piece)
-        add(column * NX + 1 - x)
+            add_half(column * NX + 1 - x, piece)
         return carry
 
     lax.fori_loop(1, NZ, lead_step, 0)
@@ -273,7 +280,8 @@
     def finish(turn, carry):
         far = z // 2
         place = (1 - far) * turn + far * (shards_each - 1 - turn)
-        turned_copy(dp * shards_each + place).wait_recv()
+        for half in range(2):
+            turned_copy(dp * shards_each + place, half).wait_recv()
 
         def part(index, carry):
             index = place * steps + index
@@ -294,7 +302,8 @@
     lax.fori_loop(0, shards_each, finish, 0)
 
     def sent(place, carry):
-        turned_copy(other * shards_each + place).wait_send()
+        for half in range(2):
+            turned_copy(other * shards_each + place, half).wait_send()
         put(place).wait()
         return carry
 
@@ -353,8 +362,8 @@
             dma(()),
             dma(()),
             dma(()),
-            dma((rows // features,)),
-            dma((rows // features,)),
+            dma((rows // features, 2)),
+            dma((rows // features, 2)),
             dma((rows // features,)),
         ],
         compiler_params=pltpu.CompilerParams(

time: 94.8 us -> 94.5 us (level)
  no operation moved by 1% of the time
where the time goes in v5:
time: 94.5 us; the launch traced here: 94.4 us
  Pallas kernels  92.1 us (97%)
  local copies, waits for them, and re-layouts  2.26 us (2%)
    pallas_call x1, Pallas kernels, fused(): pl.pallas_call(kernel, out_shape=jax.ShapeDtypeStruct((rows, BLK), bf16),...  92.1 us
    unnamed x1, local copies, waits for them, and re-layouts  2.26 us

profile of v5, /device:TPU:0, one launch (start us, length us, event | category | flops | bytes accessed | tf_op | source)
XLA Modules:
  0.0 94.4 jit_solution(3588689543910455079)
XLA Ops:
  0.0 92.1 %shard_map.64 = bf16[4096,128]{1,0:T(8,128)(2,1)} custom-call(bf16[512,1024]{1,0:T(8,128)(2,1)} %inputs.1, bf16[4096,128]{1,0:T(8,128)(2,1)} %rounding.1, s32[4096,128]{1,0:T(8,128)} %codes.1, f32[1,32]{1,0:T(1,128)} %bitcast.2, s32[1,32]{1,0:T(1,128)} %bitcast.3, bf16[512,256]{1,0:T(8,128)(2,1)} %target.1), custom_call_target="tpu_custom_call" | custom-call | tf_op jit(solution)/shard_map/pallas_call | solution.py:336
  92.1 2.3 %copy.8 = bf16[4096,128]{1,0:T(8,128)(2,1)} copy(bf16[4096,128]{1,0:T(8,128)(2,1)} %shard_map.64) | data formatting | bytes 2097152
